TPU v7x, 128 devices: a whole 4x4x4 slice. The times are simulated.
128 devices in a mesh: gx: 8 (over z, core), gy: 16 (over y, x).
Axes of the slice: x: 4, y: 4, z: 4, core: 2. Of those that a mesh axis runs over, the one named last changes fastest.
Arguments:
- displacement: float32 [3, 24, 384, 384], P(None, 'gx', 'gy'), may hold values from -1.6015 to 1.6015, as said below
- velocity: float32 [3, 24, 384, 384], P(None, 'gx', 'gy'), may hold values from -6 to 6
- energy: float32 [27, 8, 128, 128], P(None, 'gx', 'gy'), may hold values from 0.5 to 18
- mass_weight: float32 [216, 8, 128, 128], P(None, 'gx', 'gy'), may hold values from 0.002 to 0.02
- pinned_flags: int32 [3, 24, 384, 384], P(None, 'gx', 'gy'), may hold values 0 or 1
Outputs:
- acceleration: float32 [3, 24, 384, 384], P(None, 'gx', 'gy')
- velocity_new: float32 [3, 24, 384, 384], P(None, 'gx', 'gy')
- displacement_new: float32 [3, 24, 384, 384], P(None, 'gx', 'gy')
- energy_new: float32 [27, 8, 128, 128], P(None, 'gx', 'gy')
Inputs may be any that keep to these rules, and one draw needn't show every extreme that they name: Every entry of the displacement's derivative along local element coordinates stays below 0.11 in magnitude.
All inputs are finite; a program needn't handle non-finite values. No bound on the sum of `pinned_flags` on one device may be relied on, other than what follows from the above.
Results may differ from a plain program's by a relative error of at most 0.00018.
Values sent between devices are 32-bit elements; how exact they have to be, the bound alone decides.
No kernel may reach another device: no remote copies, remote signals or barrier semaphores. Data moves between devices by JAX's collectives and lax.ppermute only.
A program may use at most 128 MiB of HBM per device.

v0:
```python
from functools import partial
import math
import jax
import jax.numpy as jnp
import numpy as np
from jax import lax
from jax.sharding import PartitionSpec as P

Q = 6
ITERS = 3
HIGHEST = lax.Precision.HIGHEST
step_size = 0.05
viscosity = 0.3
gamma_less = 0.4


def shifted_2(shard, axis, by):
    devices = lax.axis_size(axis)
    return lax.ppermute(shard, axis, [(i, (i + by) % devices) for i in range(devices)])


def basis_tables():
    root_five = 1.0 / math.sqrt(5.0)
    lobatto = np.array([0.0, 0.5 - 0.5 * root_five, 0.5 + 0.5 * root_five, 1.0])
    legendre = np.array(
        [
            -0.932469514203152,
            -0.6612093864662645,
            -0.2386191860831909,
            0.2386191860831909,
            0.6612093864662645,
            0.932469514203152,
        ]
    )
    abscissa = 0.5 + 0.5 * legendre
    shape_values = np.ones((6, 4))
    shape_slopes = np.zeros((6, 4))
    for a in range(4):
        for b in range(4):
            if b != a:
                shape_values[:, a] = (
                    shape_values[:, a] * (abscissa - lobatto[b]) / (lobatto[a] - lobatto[b])
                )
        for c in range(4):
            if c != a:
                factor_term = np.ones(6) / (lobatto[a] - lobatto[c])
                for b in range(4):
                    if b != a and b != c:
                        factor_term = (
                            factor_term * (abscissa - lobatto[b]) / (lobatto[a] - lobatto[b])
                        )
                shape_slopes[:, a] = shape_slopes[:, a] + factor_term
    thermo_values = np.stack(
        [
            (1.0 - abscissa) * (1.0 - abscissa),
            2.0 * abscissa * (1.0 - abscissa),
            abscissa * abscissa,
        ],
        axis=1,
    )
    return (
        jnp.asarray(shape_values, jnp.float32),
        jnp.asarray(shape_slopes, jnp.float32),
        jnp.asarray(thermo_values, jnp.float32),
    )


def along_x(matrix, operand):
    return jnp.einsum("qa,cabgjk->cqbgjk", matrix, operand, precision=HIGHEST)


def along_y(matrix, operand):
    return jnp.einsum("qb,cabgjk->caqgjk", matrix, operand, precision=HIGHEST)


def along_z(matrix, operand):
    return jnp.einsum("qg,cabgjk->cabqjk", matrix, operand, precision=HIGHEST)


def split_nodes(operand, which_axis):
    num_cells = (operand.shape[which_axis] - 1) // 3
    outer_dims = operand.shape[:which_axis]
    inner_dims = operand.shape[which_axis + 1 :]
    head_part = lax.slice_in_dim(operand, 0, 3 * num_cells, axis=which_axis).reshape(
        outer_dims + (num_cells, 3) + inner_dims
    )
    head_part = jnp.moveaxis(head_part, which_axis + 1, which_axis)
    tail_part = lax.slice_in_dim(operand, 3, 3 * num_cells + 1, stride=3, axis=which_axis)
    return jnp.concatenate([head_part, jnp.expand_dims(tail_part, which_axis)], axis=which_axis)


def merge_nodes(operand, which_axis):
    num_cells = operand.shape[which_axis + 1]
    outer_dims = operand.shape[:which_axis]
    inner_dims = operand.shape[which_axis + 2 :]
    head_part = jnp.moveaxis(
        lax.slice_in_dim(operand, 0, 3, axis=which_axis), which_axis, which_axis + 1
    )
    head_part = head_part.reshape(outer_dims + (3 * num_cells,) + inner_dims)
    tail_part = jnp.moveaxis(
        lax.slice_in_dim(operand, 3, 4, axis=which_axis), which_axis, which_axis + 1
    )
    pad_tail = [(0, 0)] * tail_part.ndim
    pad_tail[which_axis + 1] = (0, 2)
    tail_part = jnp.pad(tail_part, pad_tail).reshape(outer_dims + (3 * num_cells,) + inner_dims)
    pad_head = [(0, 0)] * head_part.ndim
    pad_head[which_axis] = (0, 1)
    pad_shift = [(0, 0)] * head_part.ndim
    pad_shift[which_axis] = (3, 0)
    shifted = lax.slice_in_dim(jnp.pad(tail_part, pad_shift), 0, 3 * num_cells + 1, axis=which_axis)
    return jnp.pad(head_part, pad_head) + shifted


def slab_elements(slab_field):
    closed = jnp.concatenate([slab_field, slab_field[..., :1]], axis=-1)
    parts_y = split_nodes(closed, 2)
    parts_z = split_nodes(parts_y, 4)
    return jnp.moveaxis(parts_z, 4, 3)


def slab_assemble(element_field):
    parts_z = merge_nodes(jnp.moveaxis(element_field, 3, 4), 4)
    parts_y = merge_nodes(parts_z, 2)
    return jnp.concatenate([parts_y[..., :1] + parts_y[..., -1:], parts_y[..., 1:-1]], axis=-1)


def over_blocks(node_fields, cell_data, element_fn):
    num_cells = cell_data[0].shape[1]

    def one_block(block_index):
        node_start = 3 * block_index
        element_sets = tuple(
            (
                slab_elements(lax.dynamic_slice_in_dim(field_in, node_start, 4, axis=1))
                for field_in in node_fields
            )
        )
        cell_block = tuple(
            (
                lax.dynamic_index_in_dim(member, block_index, axis=1, keepdims=False)
                for member in cell_data
            )
        )
        contribution, outputs_extra = element_fn(element_sets, cell_block)
        return (slab_assemble(contribution), outputs_extra)

    node_pieces, extra_parts = lax.map(one_block, jnp.arange(num_cells, dtype=jnp.int32))
    assembled = merge_nodes(jnp.moveaxis(node_pieces, 0, 2), 1)
    return (assembled, tuple((jnp.moveaxis(member, 0, 1) for member in extra_parts)))


def thermo_interp(thermo_values, dofs):
    return along_x(thermo_values, along_y(thermo_values, along_z(thermo_values, dofs[None])))[0]


def thermo_project(thermo_values, at_quad):
    moved = thermo_values.T
    return along_x(moved, along_y(moved, along_z(moved, at_quad[None])))[0]


def force_block(element_sets, cell_block, basis_set):
    shape_values, shape_slopes, thermo_values = basis_set
    kinematic = element_sets[0]
    energy_block, weight_block = cell_block
    trailing_shape = energy_block.shape[1:]
    z_values = along_z(shape_values, kinematic)
    z_slopes = along_z(shape_slopes, kinematic)
    yz_values = along_y(shape_values, z_values)
    gradients = [
        along_x(shape_slopes, yz_values),
        along_x(shape_values, along_y(shape_slopes, z_values)),
        along_x(shape_values, along_y(shape_values, z_slopes)),
    ]
    jacobian = [[gradients[d][c] + (1.0 if c == d else 0.0) for d in range(3)] for c in range(3)]
    grad_vel = [[gradients[d][3 + c] for d in range(3)] for c in range(3)]
    cofactor = [
        [
            jacobian[(c + 1) % 3][(d + 1) % 3] * jacobian[(c + 2) % 3][(d + 2) % 3]
            - jacobian[(c + 1) % 3][(d + 2) % 3] * jacobian[(c + 2) % 3][(d + 1) % 3]
            for d in range(3)
        ]
        for c in range(3)
    ]
    determinant = (
        jacobian[0][0] * cofactor[0][0]
        + jacobian[0][1] * cofactor[0][1]
        + jacobian[0][2] * cofactor[0][2]
    )
    inverse_det = 1.0 / determinant
    spatial_grad = [
        [
            (
                grad_vel[c][0] * cofactor[e][0]
                + grad_vel[c][1] * cofactor[e][1]
                + grad_vel[c][2] * cofactor[e][2]
            )
            * inverse_det
            for e in range(3)
        ]
        for c in range(3)
    ]
    energy_quad = thermo_interp(thermo_values, energy_block.reshape((3, 3, 3) + trailing_shape))
    mass_quad = weight_block.reshape((Q, Q, Q) + trailing_shape)
    scale_quad = mass_quad * inverse_det
    stress_shape = [
        [
            viscosity * (spatial_grad[c][d] + spatial_grad[d][c])
            - (gamma_less * energy_quad if c == d else 0.0)
            for d in range(3)
        ]
        for c in range(3)
    ]
    flux = [
        [
            scale_quad
            * (
                stress_shape[c][0] * cofactor[0][f]
                + stress_shape[c][1] * cofactor[1][f]
                + stress_shape[c][2] * cofactor[2][f]
            )
            for f in range(3)
        ]
        for c in range(3)
    ]
    power_quad = jnp.zeros_like(mass_quad)
    for c in range(3):
        for f in range(3):
            power_quad = power_quad + flux[c][f] * grad_vel[c][f]
    flux_cols = [jnp.stack([flux[c][f] for c in range(3)]) for f in range(3)]
    moved = along_x(shape_slopes.T, along_y(shape_values.T, along_z(shape_values.T, flux_cols[0])))
    moved = moved + along_x(
        shape_values.T,
        along_y(shape_slopes.T, along_z(shape_values.T, flux_cols[1]))
        + along_y(shape_values.T, along_z(shape_slopes.T, flux_cols[2])),
    )
    energy_rhs = thermo_project(thermo_values, power_quad)
    lumped_mass = thermo_project(thermo_values, mass_quad)
    energy_next = energy_block + step_size * (energy_rhs / lumped_mass).reshape(energy_block.shape)
    return (-moved, (energy_next,))


def mass_block(element_sets, cell_block, basis_set):
    shape_values = basis_set[0]
    mass_quad = cell_block[0].reshape((Q, Q, Q) + cell_block[0].shape[1:])
    at_quad = (
        along_x(shape_values, along_y(shape_values, along_z(shape_values, element_sets[0])))
        * mass_quad
    )
    return (along_x(shape_values.T, along_y(shape_values.T, along_z(shape_values.T, at_quad))), ())


def extend_right(field_in):
    right_rim = shifted_2(field_in[:, :1], "gx", -1)
    wide_field = jnp.concatenate([field_in, right_rim], axis=1)
    top_rim = shifted_2(wide_field[:, :, :1], "gy", -1)
    return jnp.concatenate([wide_field, top_rim], axis=2)


def fold_back(field_in):
    upper_rim = shifted_2(field_in[:, :, -1:], "gy", 1)
    field_in = jnp.concatenate([field_in[:, :, :1] + upper_rim, field_in[:, :, 1:-1]], axis=2)
    side_rim = shifted_2(field_in[:, -1:], "gx", 1)
    return jnp.concatenate([field_in[:, :1] + side_rim, field_in[:, 1:-1]], axis=1)


def global_sum(value):
    return lax.psum(value, ("gx", "gy"))


def on_device(displacement, velocity, energy, mass_weight, pinned_flags):
    basis_set = basis_tables()
    free_mask = (1 - pinned_flags).astype(jnp.float32)
    kinematic = jnp.concatenate([displacement, velocity], axis=0)
    mass_apply = partial(mass_block, basis_set=basis_set)
    rows_x = displacement.shape[1]
    rows_y = displacement.shape[2]
    assembled, extra_parts = over_blocks(
        (extend_right(kinematic),), (energy, mass_weight), partial(force_block, basis_set=basis_set)
    )
    nodal_force = fold_back(assembled)
    owned = 1.0
    residual = free_mask * nodal_force
    energy_new = extra_parts[0]

    def local_inner(first, second):
        return jnp.sum(owned * (first * second))

    acceleration = jnp.zeros_like(residual)
    direction = residual
    norm_now = global_sum(local_inner(residual, residual))
    for iteration in range(ITERS):
        contribution = over_blocks((extend_right(direction),), (mass_weight,), mass_apply)[0]
        mass_image = free_mask * fold_back(contribution)
        step_length = norm_now / global_sum(local_inner(direction, mass_image))
        acceleration = acceleration + step_length * direction
        residual = residual - step_length * mass_image
        norm_next = global_sum(local_inner(residual, residual))
        direction = residual + norm_next / norm_now * direction
        norm_now = norm_next
    acceleration = acceleration[:, :rows_x, :rows_y]
    velocity_new = velocity + step_size * acceleration
    displacement_new = displacement + step_size * velocity_new
    return (acceleration, velocity_new, displacement_new, energy_new)


def solution(mesh):
    in_specs = (
        P(None, "gx", "gy", None),
        P(None, "gx", "gy", None),
        P(None, "gx", "gy", None),
        P(None, "gx", "gy", None),
        P(None, "gx", "gy", None),
    )
    out_specs = (
        P(None, "gx", "gy", None),
        P(None, "gx", "gy", None),
        P(None, "gx", "gy", None),
        P(None, "gx", "gy", None),
    )
    return jax.shard_map(
        on_device, mesh=mesh, in_specs=in_specs, out_specs=out_specs, check_vma=False
    )
```

profile of v0, /device:TPU:1, one launch (start us, length us, event | category | flops | bytes accessed | tf_op | source)
XLA Modules:
  0.0 1001.1 jit_solution(13770269630577380290)
XLA Ops:
  21.4 12.5 %copy.282 = f32[6,4,4,8,384]{3,2,4,1,0:T(4,128)} copy(f32[6,4,4,8,384]{4,3,2,1,0:T(8,128)S(1)} %fusion.109) | data formatting | bytes 2359296 | tf_op jit(solution)/shard_map/while/body/eval_jaxpr/slice | solution.py:84
  33.9 18.3 %copy.283 = f32[6,4,4,8,128,3]{4,5,3,2,1,0:T(4,128)S(1)} copy(f32[6,4,4,8,128,3]{3,2,5,4,1,0:T(4,128)} %bitcast.311) | data formatting | bytes 2359296 | tf_op jit(solution)/shard_map/while/body/eval_jaxpr/reshape | solution.py:84
  52.2 15.2 %slice.434 = f32[6,4,4,8,128]{4,3,2,1,0:T(8,128)S(1)} slice(f32[6,4,4,8,385]{4,3,2,1,0:T(8,128)} %pad_maximum_fusion.3), slice={[0:6:1], [0:4:1], [0:4:1], [0:8:1], [3:385:3]} | slice | bytes 786432 | tf_op jit(solution)/shard_map/while/body/eval_jaxpr/slice | solution.py:88
  86.1 9.3 fusion.18
  101.1 9.5 fusion.16
  110.6 9.5 fusion.20
  121.0 10.7 %copy_bitcast_fusion = (f32[6,6,6,6,8,128]{5,4,3,2,1,0:T(8,128)}, f32[6,6,6,6,8,128]{5,4,3,2,1,0:T(8,128)}) fusion(f32[6,6,6,8,128,6]{4,5,3,2,1,0:T(8,128)} %fusion.16, f32[6,6,6,8,128,6]{4,5,3,2,1,0:T(8,128)} %fusion.18), kind=kLoop, calls=%fused_computation.12 | loop fusion | bytes 21233664 | tf_op jit(solution)/shard_map/while/body/eval_jaxpr/qa,cabgjk->cqbgjk/transpose | solution.py:69
  144.5 11.0 %add_bitcast_fusion = (f32[6,6,6,8,128]{4,3,2,1,0:T(8,128)}, f32[1,6,6,6,8,128]{5,4,3,2,1,0:T(8,128)}, f32[1,6,6,6,8,128]{5,4,3,2,1,0:T(8,128)}, f32[1,6,6,6,8,1...) fusion(f32[1,6,6,6,8,128]{5,4,3,2,1,0:T(8,128)S(1)} %get-tuple-, ...), kind=kLoop, calls=%fused_computation.143 | loop fusion | flops 25878528 | bytes 31850496 | tf_op jit(solution)/shard_map/reshape.83
  198.9 10.8 %fusion = f32[3,4,4,8,385]{3,2,4,1,0:T(4,128)} fusion(f32[3,4,4,8,384]{3,2,4,1,0:T(4,128)} %bitcast.323, f32[3,4,4,8,384]{3,2,4,1,0:T(4,128)S(1)} %bitcast.319), kind=kLoop, calls=%fused_computation.4 | loop fusion | flops 147840 | bytes 1771008 | tf_op jit(solution)/shard_map/while/body/eval_jaxpr/add | solution.py:111
  223.7 9.2 copy.307
  270.3 10.3 %copy.315 = f32[3,4,4,8,128,3]{4,5,3,2,1,0:T(4,128)} copy(f32[3,4,4,8,128,3]{3,2,5,4,1,0:T(4,128)} %bitcast.327) | data formatting | bytes 1179648 | tf_op jit(solution)/shard_map/while/body/eval_jaxpr/reshape | solution.py:84
  328.2 12.8 %fusion.1 = f32[3,4,4,8,385]{3,2,4,1,0:T(4,128)} fusion(f32[3,4,4,8,384]{3,2,4,1,0:T(4,128)} %bitcast.320, f32[3,4,4,8,384]{3,2,4,1,0:T(4,128)} %bitcast.324), kind=kLoop, calls=%fused_computation.5 | loop fusion | flops 147840 | bytes 1771008 | tf_op jit(solution)/shard_map/while/body/eval_jaxpr/add | solution.py:111
  356.5 10.0 copy.324
  388.2 66.0 %all-reduce.36 = (f32[]{:T(128)}, f32[]{:T(128)}) all-reduce(f32[]{:T(128)} %get-tuple-element.88, f32[]{:T(128)} %get-tuple-element.87), channel_id=1, replica_groups=mesh['gx'=8,'gy'=16] {'gx','gy'}, use_global_device_ids=true, to_apply=%region_1.2 | all-reduce | flops 2 | bytes 16 | tf_op jit(solution)/shard_map/psum | solution.py:267
  457.2 62.5 %psum.44 = f32[]{:T(128)} all-reduce(f32[]{:T(128)} %get-tuple-element.114), channel_id=1, replica_groups=mesh['gx'=8,'gy'=16] {'gx','gy'}, use_global_device_ids=true, to_apply=%region_5.6 | all-reduce | flops 1 | bytes 8 | tf_op jit(solution)/shard_map/psum | solution.py:267
  544.6 10.3 %copy.333 = f32[3,4,4,8,128,3]{4,5,3,2,1,0:T(4,128)} copy(f32[3,4,4,8,128,3]{3,2,5,4,1,0:T(4,128)} %bitcast.328) | data formatting | bytes 1179648 | tf_op jit(solution)/shard_map/while/body/eval_jaxpr/reshape | solution.py:84
  605.0 12.8 %fusion.2 = f32[3,4,4,8,385]{3,2,4,1,0:T(4,128)} fusion(f32[3,4,4,8,384]{3,2,4,1,0:T(4,128)} %bitcast.321, f32[3,4,4,8,384]{3,2,4,1,0:T(4,128)} %bitcast.325), kind=kLoop, calls=%fused_computation.6 | loop fusion | flops 147840 | bytes 1771008 | tf_op jit(solution)/shard_map/while/body/eval_jaxpr/add | solution.py:111
  633.3 10.0 copy.341
  665.9 65.0 %psum.45 = f32[]{:T(128)} all-reduce(f32[]{:T(128)} %get-tuple-element.112), channel_id=1, replica_groups=mesh['gx'=8,'gy'=16] {'gx','gy'}, use_global_device_ids=true, to_apply=%region_7.8 | all-reduce | flops 1 | bytes 8 | tf_op jit(solution)/shard_map/psum | solution.py:267
  735.6 62.5 %psum.46 = f32[]{:T(128)} all-reduce(f32[]{:T(128)} %multiply_reduce_fusion), channel_id=1, replica_groups=mesh['gx'=8,'gy'=16] {'gx','gy'}, use_global_device_ids=true, to_apply=%region_9.10 | all-reduce | flops 1 | bytes 8 | tf_op jit(solution)/shard_map/psum | solution.py:267
  821.2 10.3 %copy.350 = f32[3,4,4,8,128,3]{4,5,3,2,1,0:T(4,128)} copy(f32[3,4,4,8,128,3]{3,2,5,4,1,0:T(4,128)} %bitcast.329) | data formatting | bytes 1179648 | tf_op jit(solution)/shard_map/while/body/eval_jaxpr/reshape | solution.py:84
  877.1 12.9 %fusion.3 = f32[3,4,4,8,385]{3,2,4,1,0:T(4,128)} fusion(f32[3,4,4,8,384]{3,2,4,1,0:T(4,128)} %bitcast.322, f32[3,4,4,8,384]{3,2,4,1,0:T(4,128)} %bitcast.326), kind=kLoop, calls=%fused_computation.7 | loop fusion | flops 147840 | bytes 1771008 | tf_op jit(solution)/shard_map/while/body/eval_jaxpr/add | solution.py:111
  905.4 9.1 copy.358
  933.3 65.1 %psum.47 = f32[]{:T(128)} all-reduce(f32[]{:T(128)} %fusion.140), channel_id=1, replica_groups=mesh['gx'=8,'gy'=16] {'gx','gy'}, use_global_device_ids=true, to_apply=%region_11.12 | all-reduce | flops 1 | bytes 8 | tf_op jit(solution)/shard_map/psum | solution.py:267
  (293 shorter events, 456.6 us)
Async XLA Ops:
  0.6 13.7 %copy-start.25 = (f32[6,3,1,1,1]{0,1,4,3,2:T(4,128)S(1)}, f32[6,3,1,1,1]{0,1,4,3,2:T(4,128)}, u32[]{:S(2)}) copy-start(f32[6,3,1,1,1]{0,1,4,3,2:T(4,128)} %constant.174) | copy-start | bytes 220
  2.7 6.7 collective-permute-start
  9.4 6.4 collective-permute-start.1
  33.9 33.5 %copy-start.18 = (f32[6,4,1,1,1,1]{0,1,5,4,3,2:T(4,128)S(1)}, f32[6,4,1,1,1,1]{0,1,5,4,3,2:T(4,128)}, u32[]{:S(2)}) copy-start(f32[6,4,1,1,1,1]{0,1,5,4,3,2:T(4,128)} %constant.172) | copy-start | bytes 292
  235.7 10.8 %copy-start.3 = (s32[3,3,24,384]{3,2,1,0:T(8,128)S(1)}, s32[3,3,24,384]{3,2,1,0:T(8,128)}, u32[]{:S(2)}) copy-start(s32[3,3,24,384]{3,2,1,0:T(8,128)} %param.12) | copy-start | bytes 995332
  235.8 18.2 %copy-start.2 = (f32[216,1,8,128]{3,2,1,0:T(8,128)S(1)}, f32[216,1,8,128]{3,2,1,0:T(8,128)}, u32[]{:S(2)}) copy-start(f32[216,1,8,128]{3,2,1,0:T(8,128)} %param.11) | copy-start | bytes 2654212
  235.8 6.0 collective-permute-start.2
  241.9 4.6 collective-permute-start.3
  246.6 5.5 collective-permute-start.4
  252.2 2.7 collective-permute-start.5
  376.8 6.3 collective-permute-start.6
  383.1 4.2 collective-permute-start.7
  387.4 66.8 %copy-start.22 = (f32[3,1,24,384]{3,2,1,0:T(8,128)}, f32[3,1,24,384]{3,2,1,0:T(8,128)S(1)}, u32[]{:S(2)}) copy-start(f32[3,1,24,384]{3,2,1,0:T(8,128)S(1)} %maximum_add_fusion.2) | copy-start | bytes 331780
  521.1 4.2 collective-permute-start.8
  525.3 3.2 collective-permute-start.9
  654.9 6.7 collective-permute-start.10
  661.7 3.5 collective-permute-start.11
  799.5 4.2 collective-permute-start.12
  803.7 3.9 collective-permute-start.13
  922.4 6.0 collective-permute-start.14
  923.4 9.2 copy-start.23
  923.4 76.3 %copy-start.19 = (f32[3,3,24,384]{3,2,1,0:T(8,128)S(1)}, f32[3,3,24,384]{3,2,1,0:T(8,128)}, u32[]{:S(2)}) copy-start(f32[3,3,24,384]{3,2,1,0:T(8,128)} %param.8) | copy-start | bytes 995332
  923.4 76.3 %copy-start.20 = (f32[3,3,24,384]{3,2,1,0:T(8,128)S(1)}, f32[3,3,24,384]{3,2,1,0:T(8,128)}, u32[]{:S(2)}) copy-start(f32[3,3,24,384]{3,2,1,0:T(8,128)} %param.9) | copy-start | bytes 995332
  928.4 3.5 collective-permute-start.15
  (24 other events, 90.7 us)
where the time goes:
time: 1010 us; the launch traced here: 1000 us
  local copies, waits for them, and re-layouts  364 us (36%)
  blocking collectives  321 us (32%)
  matrix products  153 us (15%)
  other arithmetic  88.8 us (9%)
  waiting for transfers between devices  40 us (4%)
  starting transfers between devices  25.2 us (2%)
    psum x5, blocking collectives, global_sum(): return lax.psum(value, ('gx', 'gy'))  321 us
    transpose x16, local copies, waits for them, and re-layouts, merge_nodes(): jnp.moveaxis(lax.slice_in_dim(operand, 0, 3, axis=which_axis), which_axis...  104 us
    dot_general x14, matrix products, along_x(): return jnp.einsum('qa,cabgjk->cqbgjk', matrix, operand, precision=HIGHEST)  55.3 us
    dot_general x15, matrix products, along_y(): return jnp.einsum('qb,cabgjk->caqgjk', matrix, operand, precision=HIGHEST)  50.4 us
    reshape x8, local copies, waits for them, and re-layouts, split_nodes(): lax.slice_in_dim(operand, 0, 3 * num_cells, axis=which_axis)  50.1 us
    add x12, other arithmetic, merge_nodes(): return jnp.pad(head_part, pad_head) + shifted  50 us
    dot_general x14, matrix products, along_z(): return jnp.einsum('qg,cabgjk->cabqjk', matrix, operand, precision=HIGHEST)  47.1 us
    slice x8, local copies, waits for them, and re-layouts, split_nodes(): lax.slice_in_dim(operand, 3, 3 * num_cells + 1, stride=3, axis=which_axis)  46.5 us
  transfers between devices with their start and end apart: 16, of which 13 were waited for; matrix products, arithmetic and copies ran while one was open for 1% of the time, Pallas kernels for 0%

commit v1 on v0

--- a/solution.py
+++ b/solution.py
@@ -264,7 +264,13 @@
 
 
 def global_sum(value):
-    return lax.psum(value, ("gx", "gy"))
+
+    def test_arrays(local, axis_tag, net_axis):
+        for jj in (net_axis, axis_tag):
+            local = lax.psum(local, axis_name=jj)
+        return local
+
+    return test_arrays(value, "gx", "gy")
 
 
 def on_device(displacement, velocity, energy, mass_weight, pinned_flags):

time: 1010 us -> 958 us (0.949)
  blocking collectives: 321 us -> 259 us
    psum x5 -> x10, blocking collectives: 321 us -> 259 us  [test_arrays(): local = lax.psum(local, axis_name=jj)]
    unnamed x73 -> x81, local copies, waits for them, and re-layouts: 39.7 us -> 42.1 us
  transfers between devices with their start and end apart: 16 -> 16, of which waited for: 13 -> 14; matrix products, arithmetic and copies ran while one was open for 1% -> 1% of each run, Pallas kernels for 0% -> 0%
where the time goes in v1:
time: 958 us; the launch traced here: 946 us
  local copies, waits for them, and re-layouts  366 us (38%)
  blocking collectives  259 us (27%)
  matrix products  154 us (16%)
  other arithmetic  92.9 us (10%)
  waiting for transfers between devices  40.5 us (4%)
  starting transfers between devices  25.1 us (3%)
    psum x10, blocking collectives, test_arrays(): local = lax.psum(local, axis_name=jj)  259 us
    transpose x16, local copies, waits for them, and re-layouts, merge_nodes(): jnp.moveaxis(lax.slice_in_dim(operand, 0, 3, axis=which_axis), which_axis...  102 us
    dot_general x14, matrix products, along_x(): return jnp.einsum('qa,cabgjk->cqbgjk', matrix, operand, precision=HIGHEST)  56.4 us
    dot_general x15, matrix products, along_y(): return jnp.einsum('qb,cabgjk->caqgjk', matrix, operand, precision=HIGHEST)  50.7 us
    reshape x8, local copies, waits for them, and re-layouts, split_nodes(): lax.slice_in_dim(operand, 0, 3 * num_cells, axis=which_axis)  50.1 us
    add x12, other arithmetic, merge_nodes(): return jnp.pad(head_part, pad_head) + shifted  49.9 us
    dot_general x14, matrix products, along_z(): return jnp.einsum('qg,cabgjk->cabqjk', matrix, operand, precision=HIGHEST)  47.3 us
    slice x8, local copies, waits for them, and re-layouts, split_nodes(): lax.slice_in_dim(operand, 3, 3 * num_cells + 1, stride=3, axis=which_axis)  46 us
  transfers between devices with their start and end apart: 16, of which 14 were waited for; matrix products, arithmetic and copies ran while one was open for 1% of the time, Pallas kernels for 0%

profile of v1, /device:TPU:1, one launch (start us, length us, event | category | flops | bytes accessed | tf_op | source)
XLA Modules:
  0.0 946.4 jit_solution(11480510170285200875)
XLA Ops:
  20.2 12.5 %copy.282 = f32[6,4,4,8,384]{3,2,4,1,0:T(4,128)} copy(f32[6,4,4,8,384]{4,3,2,1,0:T(8,128)S(1)} %fusion.109) | data formatting | bytes 2359296 | tf_op jit(solution)/shard_map/while/body/eval_jaxpr/slice | solution.py:84
  32.7 18.3 %copy.283 = f32[6,4,4,8,128,3]{4,5,3,2,1,0:T(4,128)S(1)} copy(f32[6,4,4,8,128,3]{3,2,5,4,1,0:T(4,128)} %bitcast.311) | data formatting | bytes 2359296 | tf_op jit(solution)/shard_map/while/body/eval_jaxpr/reshape | solution.py:84
  51.0 15.0 %slice.434 = f32[6,4,4,8,128]{4,3,2,1,0:T(8,128)S(1)} slice(f32[6,4,4,8,385]{4,3,2,1,0:T(8,128)} %pad_maximum_fusion.3), slice={[0:6:1], [0:4:1], [0:4:1], [0:8:1], [3:385:3]} | slice | bytes 786432 | tf_op jit(solution)/shard_map/while/body/eval_jaxpr/slice | solution.py:88
  119.8 10.7 %copy_bitcast_fusion = (f32[6,6,6,6,8,128]{5,4,3,2,1,0:T(8,128)}, f32[6,6,6,6,8,128]{5,4,3,2,1,0:T(8,128)}) fusion(f32[6,6,6,8,128,6]{4,5,3,2,1,0:T(8,128)} %fusion.16, f32[6,6,6,8,128,6]{4,5,3,2,1,0:T(8,128)} %fusion.18), kind=kLoop, calls=%fused_computation.12 | loop fusion | bytes 21233664 | tf_op jit(solution)/shard_map/while/body/eval_jaxpr/qa,cabgjk->cqbgjk/transpose | solution.py:69
  144.1 11.7 %add_bitcast_fusion = (f32[6,6,6,8,128]{4,3,2,1,0:T(8,128)}, f32[1,6,6,6,8,128]{5,4,3,2,1,0:T(8,128)}, f32[1,6,6,6,8,128]{5,4,3,2,1,0:T(8,128)}, f32[1,6,6,6,8,1...) fusion(f32[1,6,6,6,8,128]{5,4,3,2,1,0:T(8,128)} %get-tuple-elem, ...), kind=kLoop, calls=%fused_computation.143 | loop fusion | flops 25878528 | bytes 31850496 | tf_op jit(solution)/shard_map/reshape.83
  200.5 10.8 %fusion = f32[3,4,4,8,385]{3,2,4,1,0:T(4,128)} fusion(f32[3,4,4,8,384]{3,2,4,1,0:T(4,128)} %bitcast.323, f32[3,4,4,8,384]{3,2,4,1,0:T(4,128)S(1)} %bitcast.319), kind=kLoop, calls=%fused_computation.4 | loop fusion | flops 147840 | bytes 1771008 | tf_op jit(solution)/shard_map/while/body/eval_jaxpr/add | solution.py:111
  272.9 10.3 %copy.315 = f32[3,4,4,8,128,3]{4,5,3,2,1,0:T(4,128)} copy(f32[3,4,4,8,128,3]{3,2,5,4,1,0:T(4,128)} %bitcast.327) | data formatting | bytes 1179648 | tf_op jit(solution)/shard_map/while/body/eval_jaxpr/reshape | solution.py:84
  331.0 12.8 %fusion.1 = f32[3,4,4,8,385]{3,2,4,1,0:T(4,128)} fusion(f32[3,4,4,8,384]{3,2,4,1,0:T(4,128)} %bitcast.320, f32[3,4,4,8,384]{3,2,4,1,0:T(4,128)} %bitcast.324), kind=kLoop, calls=%fused_computation.5 | loop fusion | flops 147840 | bytes 1771008 | tf_op jit(solution)/shard_map/while/body/eval_jaxpr/add | solution.py:111
  359.3 10.0 %copy.324 = f32[3,4,8,3,385]{4,1,3,2,0:T(4,128)} copy(f32[3,4,8,3,385]{2,3,4,1,0:T(4,128)} %slice_bitcast_fusion.2) | data formatting | bytes 887040 | tf_op jit(solution)/shard_map/while/body/eval_jaxpr/transpose | solution.py:96
  391.0 30.6 %all-reduce.36 = (f32[]{:T(128)}, f32[]{:T(128)}) all-reduce(f32[]{:T(128)} %get-tuple-element.88, f32[]{:T(128)} %get-tuple-element.87), channel_id=1, replica_groups=mesh['gx'=8,'gy'=16] {'gy'}, use_global_device_ids=true, to_apply=%region_1.2 | all-reduce | flops 2 | bytes 16 | tf_op jit(solution)/shard_map/psum | solution.py:270
  421.6 23.9 %all-reduce.37 = (f32[]{:T(128)}, f32[]{:T(128)}) all-reduce(f32[]{:T(128)} %get-tuple-element.89, f32[]{:T(128)} %get-tuple-element.90), channel_id=1, replica_groups=mesh['gx'=8,'gy'=16] {'gx'}, use_global_device_ids=true, to_apply=%region_2.3 | all-reduce | flops 2 | bytes 16 | tf_op jit(solution)/shard_map/psum | solution.py:270
  448.5 29.5 %psum.88 = f32[]{:T(128)} all-reduce(f32[]{:T(128)} %get-tuple-element.116), channel_id=1, replica_groups=mesh['gx'=8,'gy'=16] {'gy'}, use_global_device_ids=true, to_apply=%region_7.8 | all-reduce | flops 1 | bytes 8 | tf_op jit(solution)/shard_map/psum | solution.py:270
  478.0 20.1 %psum.89 = f32[]{:T(128)} all-reduce(f32[]{:T(128)} %psum.88), channel_id=1, replica_groups=mesh['gx'=8,'gy'=16] {'gx'}, use_global_device_ids=true, to_apply=%region_8.9 | all-reduce | flops 1 | bytes 8 | tf_op jit(solution)/shard_map/psum | solution.py:270
  522.6 10.3 %copy.333 = f32[3,4,4,8,128,3]{4,5,3,2,1,0:T(4,128)} copy(f32[3,4,4,8,128,3]{3,2,5,4,1,0:T(4,128)} %bitcast.328) | data formatting | bytes 1179648 | tf_op jit(solution)/shard_map/while/body/eval_jaxpr/reshape | solution.py:84
  583.0 12.8 %fusion.2 = f32[3,4,4,8,385]{3,2,4,1,0:T(4,128)} fusion(f32[3,4,4,8,384]{3,2,4,1,0:T(4,128)} %bitcast.321, f32[3,4,4,8,384]{3,2,4,1,0:T(4,128)} %bitcast.325), kind=kLoop, calls=%fused_computation.6 | loop fusion | flops 147840 | bytes 1771008 | tf_op jit(solution)/shard_map/while/body/eval_jaxpr/add | solution.py:111
  611.3 10.0 %copy.341 = f32[3,4,8,3,385]{4,1,3,2,0:T(4,128)} copy(f32[3,4,8,3,385]{2,3,4,1,0:T(4,128)} %slice_bitcast_fusion.1) | data formatting | bytes 887040 | tf_op jit(solution)/shard_map/while/body/eval_jaxpr/transpose | solution.py:96
  644.4 30.3 %psum.90 = f32[]{:T(128)} all-reduce(f32[]{:T(128)} %get-tuple-element.114), channel_id=1, replica_groups=mesh['gx'=8,'gy'=16] {'gy'}, use_global_device_ids=true, to_apply=%region_10.11 | all-reduce | flops 1 | bytes 8 | tf_op jit(solution)/shard_map/psum | solution.py:270
  674.7 22.2 %psum.91 = f32[]{:T(128)} all-reduce(f32[]{:T(128)} %psum.90), channel_id=1, replica_groups=mesh['gx'=8,'gy'=16] {'gx'}, use_global_device_ids=true, to_apply=%region_11.12 | all-reduce | flops 1 | bytes 8 | tf_op jit(solution)/shard_map/psum | solution.py:270
  701.9 29.5 %psum.92 = f32[]{:T(128)} all-reduce(f32[]{:T(128)} %multiply_reduce_fusion), channel_id=1, replica_groups=mesh['gx'=8,'gy'=16] {'gy'}, use_global_device_ids=true, to_apply=%region_13.14 | all-reduce | flops 1 | bytes 8 | tf_op jit(solution)/shard_map/psum | solution.py:270
  734.0 20.1 %psum.93 = f32[]{:T(128)} all-reduce(f32[]{:T(128)} %psum.92), channel_id=1, replica_groups=mesh['gx'=8,'gy'=16] {'gx'}, use_global_device_ids=true, to_apply=%region_14.15 | all-reduce | flops 1 | bytes 8 | tf_op jit(solution)/shard_map/psum | solution.py:270
  777.2 10.3 %copy.350 = f32[3,4,4,8,128,3]{4,5,3,2,1,0:T(4,128)} copy(f32[3,4,4,8,128,3]{3,2,5,4,1,0:T(4,128)} %bitcast.329) | data formatting | bytes 1179648 | tf_op jit(solution)/shard_map/while/body/eval_jaxpr/reshape | solution.py:84
  833.1 12.8 %fusion.3 = f32[3,4,4,8,385]{3,2,4,1,0:T(4,128)} fusion(f32[3,4,4,8,384]{3,2,4,1,0:T(4,128)} %bitcast.322, f32[3,4,4,8,384]{3,2,4,1,0:T(4,128)} %bitcast.326), kind=kLoop, calls=%fused_computation.7 | loop fusion | flops 147840 | bytes 1771008 | tf_op jit(solution)/shard_map/while/body/eval_jaxpr/add | solution.py:111
  890.6 30.3 %psum.94 = f32[]{:T(128)} all-reduce(f32[]{:T(128)} %fusion.140), channel_id=1, replica_groups=mesh['gx'=8,'gy'=16] {'gy'}, use_global_device_ids=true, to_apply=%region_16.17 | all-reduce | flops 1 | bytes 8 | tf_op jit(solution)/shard_map/psum | solution.py:270
  921.6 22.2 %psum.95 = f32[]{:T(128)} all-reduce(f32[]{:T(128)} %psum.94), channel_id=1, replica_groups=mesh['gx'=8,'gy'=16] {'gx'}, use_global_device_ids=true, to_apply=%region_17.18 | all-reduce | flops 1 | bytes 8 | tf_op jit(solution)/shard_map/psum | solution.py:270
  (306 shorter events, 510.5 us)
Async XLA Ops:
  0.6 13.7 %copy-start.29 = (f32[6,3,1,1,1]{0,1,4,3,2:T(4,128)S(1)}, f32[6,3,1,1,1]{0,1,4,3,2:T(4,128)}, u32[]{:S(2)}) copy-start(f32[6,3,1,1,1]{0,1,4,3,2:T(4,128)} %constant.174) | copy-start | bytes 220
  2.7 6.7 collective-permute-start
  9.4 7.5 collective-permute-start.1
  32.7 33.3 %copy-start.22 = (f32[6,4,1,1,1,1]{0,1,5,4,3,2:T(4,128)S(1)}, f32[6,4,1,1,1,1]{0,1,5,4,3,2:T(4,128)}, u32[]{:S(2)}) copy-start(f32[6,4,1,1,1,1]{0,1,5,4,3,2:T(4,128)} %constant.172) | copy-start | bytes 292
  239.0 17.1 %copy-start.3 = (f32[216,1,8,128]{3,2,1,0:T(8,128)S(1)}, f32[216,1,8,128]{3,2,1,0:T(8,128)}, u32[]{:S(2)}) copy-start(f32[216,1,8,128]{3,2,1,0:T(8,128)} %param.11) | copy-start | bytes 2654212
  239.0 6.0 collective-permute-start.2
  245.1 4.1 collective-permute-start.3
  249.2 5.5 collective-permute-start.4
  254.8 2.7 collective-permute-start.5
  379.6 6.0 collective-permute-start.6
  385.7 4.5 collective-permute-start.7
  390.2 55.3 %copy-start.26 = (f32[3,1,24,384]{3,2,1,0:T(8,128)}, f32[3,1,24,384]{3,2,1,0:T(8,128)S(1)}, u32[]{:S(2)}) copy-start(f32[3,1,24,384]{3,2,1,0:T(8,128)S(1)} %maximum_add_fusion.2) | copy-start | bytes 331780
  499.6 4.2 collective-permute-start.8
  503.8 2.7 collective-permute-start.9
  632.9 67.0 %copy-start.30 = (f32[6,3,1,1,1]{0,1,4,3,2:T(4,128)S(1)}, f32[6,3,1,1,1]{0,1,4,3,2:T(4,128)}, u32[]{:S(2)}) copy-start(f32[6,3,1,1,1]{0,1,4,3,2:T(4,128)} %constant.174) | copy-start | bytes 220
  632.9 6.0 collective-permute-start.10
  639.0 4.0 collective-permute-start.11
  756.6 4.2 collective-permute-start.12
  760.8 2.8 collective-permute-start.13
  879.9 6.0 collective-permute-start.14
  881.5 39.4 %copy-start.27 = (f32[27,1,8,128]{3,2,1,0:T(8,128)S(1)}, f32[27,1,8,128]{3,2,1,0:T(8,128)}, u32[]{:S(2)}) copy-start(f32[27,1,8,128]{3,2,1,0:T(8,128)} %param.10) | copy-start | bytes 331780
  881.5 63.6 %copy-start.23 = (f32[3,3,24,384]{3,2,1,0:T(8,128)S(1)}, f32[3,3,24,384]{3,2,1,0:T(8,128)}, u32[]{:S(2)}) copy-start(f32[3,3,24,384]{3,2,1,0:T(8,128)} %param.8) | copy-start | bytes 995332
  881.5 63.6 %copy-start.24 = (f32[3,3,24,384]{3,2,1,0:T(8,128)S(1)}, f32[3,3,24,384]{3,2,1,0:T(8,128)}, u32[]{:S(2)}) copy-start(f32[3,3,24,384]{3,2,1,0:T(8,128)} %param.9) | copy-start | bytes 995332
  886.0 3.9 collective-permute-start.15
  (28 other events, 116.4 us)
